TPU v7x, 32 devices: a whole 2x2x4 slice. The times are simulated.
32 devices in a mesh: seq: 4 (over y, core), batch: 8 (over z, x).
Axes of the slice: x: 2, y: 2, z: 4, core: 2. Of those that a mesh axis runs over, the one named last changes fastest.
Arguments:
- tower: bfloat16 [6144, 1536], P(('batch', 'seq')), parts along dimension 0, may hold values from -6 to 6
- dna: int32 [6144, 128], P(('batch', 'seq')), parts along dimension 0, may hold values from 0 to 3
- dna_weight: float32 [4, 1536], replicated, may hold values from -3 to 3
- conv_gain: float32 [1536], replicated, may hold values from 0.25 to 1.75
- depthwise_kernel: float32 [5, 1536], replicated, may hold values from -2.5 to 2.5
- attn_gain: float32 [1536], replicated, may hold values from 0.25 to 1.75
- query_weight: bfloat16 [1536, 1024], P('seq'), may hold values from -1 to 1
- key_weight: bfloat16 [1536, 128], P('seq'), may hold values from -1 to 1
- value_weight: bfloat16 [1536, 192], P('seq'), may hold values from -0.15625 to 0.15625
- out_weight: bfloat16 [1536, 1536], P('seq'), may hold values from -0.15625 to 0.15625
- pair_in_weight: bfloat16 [1536, 256], replicated, may hold values from -0.15625 to 0.15625
- pair_weight: bfloat16 [128, 128], replicated, may hold values from -0.5 to 0.5
Outputs:
- stream_out: bfloat16 [6144, 1536], P(('batch', 'seq')), parts along dimension 0
- pair: bfloat16 [384, 48, 128], P(('batch', 'seq')), parts along dimension 0
There are 8 independent parts, one for each index of `batch`. A program takes and returns all parts, laid end to end along the dimension named above; an argument that names none is the same for every part. Nothing has to cross between parts.
All inputs are finite; a program needn't handle non-finite values.
Results may differ from a plain program's by a relative error of at most 0.013.
Values may be sent and summed in bfloat16 or wider, within the bound.
A program may use at most 64 MiB of HBM per device.

v0:
```python
import math

import jax
import jax.numpy as jnp
from jax import lax
from jax.sharding import PartitionSpec as P

H = 8
DK = 128
DV = 192
BASES = 128
POOL = 16
KERNEL_TAPS = 5
DILATION_STEP = 4


def extended(cells, sides, width):
    for axis, dim in sides:
        count = lax.axis_size(axis)
        ends = count - 1
        head = lax.slice_in_dim(cells, 0, width, axis=dim)
        tail = lax.slice_in_dim(cells, cells.shape[dim] - width, cells.shape[dim], axis=dim)
        cells = jnp.concatenate(
            [
                lax.ppermute(tail, axis, [(i, (i + 1) % count) for i in range(ends)]),
                cells,
                lax.ppermute(head, axis, [((i + 1) % count, i) for i in range(ends)]),
            ],
            axis=dim,
        )
    return cells


def rms_norm(values, gain):
    wide = values.astype(jnp.float32)
    return wide * lax.rsqrt(jnp.mean(wide * wide, axis=-1, keepdims=True) + 1e-06) * gain


def block_length(span):
    pieces_count = 1
    while span // pieces_count > 1024 or span % pieces_count != 0:
        pieces_count = pieces_count + 1
    return span // pieces_count


def local(
    tower,
    dna,
    dna_weight,
    conv_gain,
    depthwise_kernel,
    attn_gain,
    query_weight,
    key_weight,
    value_weight,
    out_weight,
    pair_in_weight,
    pair_weight,
):
    count_of_rows = tower.shape[0]
    channels = tower.shape[1]
    counts = jnp.sum(
        (dna[:, :, None] == jnp.arange(4, dtype=jnp.int32)[None, None, :]).astype(jnp.float32),
        axis=1,
    )
    composition = (counts - BASES / 4.0) * (4.0 / math.sqrt(3.0 * BASES))
    stream = tower.astype(jnp.float32) + jnp.dot(
        composition, dna_weight, precision=lax.Precision.HIGHEST
    )
    normed = rms_norm(stream, conv_gain).astype(jnp.bfloat16)
    kernel_reach = DILATION_STEP * (KERNEL_TAPS - 1) // 2
    padded_rows = extended(normed, (("seq", 0),), kernel_reach).astype(jnp.float32)
    convolved_rows = jnp.zeros_like(stream)
    for kernel_tap in range(KERNEL_TAPS):
        convolved_rows = (
            convolved_rows
            + depthwise_kernel[kernel_tap]
            * padded_rows[kernel_tap * DILATION_STEP : kernel_tap * DILATION_STEP + count_of_rows]
        )
    conv_out = (stream + jax.nn.gelu(convolved_rows)).astype(jnp.bfloat16)
    attn_in = rms_norm(conv_out, attn_gain).astype(jnp.bfloat16)
    pieces = (
        lax.all_gather(query_weight, "seq", axis=0, tiled=True),
        lax.all_gather(key_weight, "seq", axis=0, tiled=True),
        lax.all_gather(value_weight, "seq", axis=0, tiled=True),
    )
    columns = attn_in
    query_sum, key_sum, value_sum = tuple(
        (jnp.dot(columns, piece, preferred_element_type=jnp.float32) for piece in pieces)
    )
    flat_queries = query_sum.astype(jnp.bfloat16).reshape(count_of_rows * H, DK)
    keys_local = key_sum.astype(jnp.bfloat16)
    values_local = value_sum.astype(jnp.bfloat16)
    scale = 1.0 / math.sqrt(DK)
    start_state = (
        jnp.full((count_of_rows * H,), -1e30, jnp.float32),
        jnp.zeros((count_of_rows * H,), jnp.float32),
        jnp.zeros((count_of_rows * H, DV), jnp.float32),
    )
    key_piece = lax.all_gather(keys_local, "seq", axis=0, tiled=True)
    value_piece = lax.all_gather(values_local, "seq", axis=0, tiled=True)
    span = key_piece.shape[0]
    block = block_length(span)
    key_slabs = key_piece.reshape(span // block, block, DK)
    value_slabs = value_piece.reshape(span // block, block, DV)

    def step_block(state, slabs):
        running_max, running_sum, running_acc = state
        key_slab, value_slab = slabs
        scores = (
            lax.dot_general(
                key_slab, flat_queries, (((1,), (1,)), ((), ())), preferred_element_type=jnp.float32
            )
            * scale
        )
        new_max = jnp.maximum(running_max, jnp.max(scores, axis=0))
        correct = jnp.exp(running_max - new_max)
        expo = jnp.exp(scores - new_max[None, :])
        new_sum = running_sum * correct + jnp.sum(expo, axis=0)
        summed = lax.dot_general(
            expo.astype(jnp.bfloat16),
            value_slab,
            (((0,), (0,)), ((), ())),
            preferred_element_type=jnp.float32,
        )
        new_acc = running_acc * correct[:, None] + summed
        return ((new_max, new_sum, new_acc), None)

    result, unused = lax.scan(step_block, start_state, (key_slabs, value_slabs))
    final_max, final_sum, final_acc = result
    context = (final_acc / final_sum[:, None]).reshape(count_of_rows, H * DV).astype(jnp.bfloat16)
    columns = context
    projected = jnp.dot(
        columns,
        lax.all_gather(out_weight, "seq", axis=0, tiled=True),
        preferred_element_type=jnp.float32,
    )
    stream_out = (conv_out.astype(jnp.float32) + projected).astype(jnp.bfloat16)
    pooled = jnp.mean(
        stream_out.astype(jnp.float32).reshape(count_of_rows // POOL, POOL, channels), axis=1
    ).astype(jnp.bfloat16)
    pair_width = pair_weight.shape[0]
    own_rows = count_of_rows // POOL
    all_pooled = lax.all_gather(pooled, "seq", axis=0, tiled=True)
    all_features = jnp.dot(all_pooled, pair_in_weight, preferred_element_type=jnp.float32).astype(
        jnp.bfloat16
    )
    own_features = lax.dynamic_slice_in_dim(
        all_features, lax.axis_index("seq") * own_rows, own_rows, 0
    )
    left = own_features[:, :pair_width]
    right = all_features[:, pair_width:]
    left_wide = left.astype(jnp.float32)
    right_wide = right.astype(jnp.float32)
    outer = (left_wide[:, None, :] * right_wide[None, :, :]).astype(jnp.bfloat16)
    all_rows = right.shape[0]
    mixed = jnp.dot(
        outer.reshape(own_rows * all_rows, pair_width),
        pair_weight,
        preferred_element_type=jnp.float32,
    ).reshape(own_rows, all_rows, pair_width)
    pair = (mixed + left_wide[:, None, :] + right_wide[None, :, :]).astype(jnp.bfloat16)
    return (stream_out, pair)


def solution(mesh):
    in_specs = (
        P(("batch", "seq"), None),
        P(("batch", "seq"), None),
        P(),
        P(),
        P(),
        P(),
        P("seq", None),
        P("seq", None),
        P("seq", None),
        P("seq", None),
        P(),
        P(),
    )
    out_specs = (P(("batch", "seq"), None), P(("batch", "seq"), None, None))
    return jax.shard_map(local, mesh=mesh, in_specs=in_specs, out_specs=out_specs, check_vma=False)
```

profile of v0, /device:TPU:0, one launch (start us, length us, event | category | flops | bytes accessed | tf_op | source)
XLA Modules:
  0.0 102.0 jit_solution(4939696690579067580)
XLA Ops:
  7.3 0.7 all-gather.4.cloned.1.call-update
  8.0 0.7 all-gather.6.cloned.1.call-update
  8.9 1.3 %multiply_reduce_fusion.1 = (f32[192]{0:T(256)S(1)}, f32[192,1536]{1,0:T(8,128)S(1)}) fusion(f32[4,1536]{1,0:T(4,128)S(1)} %copy-done.9, f32[192,4]{0,1:T(4,128)S(1)} %convert_reduce_fusion.1, bf16[192,1536]{1,0:T(8,128)(2,1)S(1)} %copy-done.1), kind=kOutput, calls=%fused_computation.39 | convolution fusion | flops 15336768 | bytes 1797888 | tf_op jit(solution)/shard_map/dot_general | solution.py:67
  10.4 0.6 fusion.42
  11.1 2.9 %collective-permute-start = (bf16[8,1536]{1,0:T(8,128)(2,1)}, bf16[8,1536]{1,0:T(8,128)(2,1)}, u32[]{:S(2)}, u32[]{:S(2)}) collective-permute-start(bf16[8,1536]{1,0:T(8,128)(2,1)} %get-tuple-element.30), channel_id=1, source_target_pairs={{0,8},{8,16},{16,24},{1,9},{9,17},{17,25},{2,10},{10,18},{18,26},{... | collective-permute-start | bytes 73736 | tf_op jit(solution)/shard_map/ppermute | solution.py:25
  14.0 1.3 %collective-permute-start.1 = (bf16[8,1536]{1,0:T(8,128)(2,1)}, bf16[8,1536]{1,0:T(8,128)(2,1)}, u32[]{:S(2)}, u32[]{:S(2)}) collective-permute-start(bf16[8,1536]{1,0:T(8,128)(2,1)} %get-tuple-element.31), channel_id=1, source_target_pairs={{8,0},{16,8},{24,16},{9,1},{17,9},{25,17},{10,2},{18,10},{26,18},{... | collective-permute-start | bytes 73736 | tf_op jit(solution)/shard_map/ppermute | solution.py:27
  15.3 10.8 %all_gather.21 = bf16[1536,128]{1,0:T(8,128)(2,1)S(1)} all-gather(bf16[384,128]{1,0:T(8,128)(2,1)S(1)} %copy-done.5), channel_id=1, replica_groups=mesh['seq'=4,'batch'=8] {'seq'}, dimensions={0}, use_global_device_ids=true | all-gather | bytes 491520 | tf_op jit(solution)/shard_map/all_gather | solution.py:84
  26.1 11.2 %all_gather.24 = bf16[1536,192]{0,1:T(8,128)(2,1)S(1)} all-gather(bf16[384,192]{0,1:T(8,128)(2,1)S(1)} %copy-done.3), channel_id=1, replica_groups=mesh['seq'=4,'batch'=8] {'seq'}, dimensions={0}, use_global_device_ids=true | all-gather | bytes 737280 | tf_op jit(solution)/shard_map/all_gather | solution.py:85
  37.3 0.7 slice_reduce_fusion.4
  38.0 0.9 maximum_convert_fusion
  39.0 1.1 %fusion.17 = (f32[192]{0:T(256)S(1)}, bf16[192,1536]{1,0:T(8,128)(2,1)S(1)}) fusion(f32[192,1536]{1,0:T(8,128)S(1)} %get-tuple-element.35, f32[208,1536]{1,0:T(8,128)S(1)} %maximum_convert_fusion, f32[1536]{0:T(1024)S(1)} %copy-done.7, f32[1536]{0:T(1024)S(1)} %copy-done.8, f32[1536]{0:T(1024)S(1)} %get-tuple-element.17, f32[1536]{0:T(1024)S(1)} %copy-done.6, ...), kind=kLoop, calls=%fused_computation.25 | loop fusion | flops 6487872 | bytes 7699200 | tf_op jit(solution)/shard_map/reduce_sum | solution.py:36
  40.1 0.4 convolution_convert_fusion.2
  40.5 5.6 %all_gather.22 = bf16[768,128]{1,0:T(8,128)(2,1)S(1)} all-gather(bf16[192,128]{1,0:T(8,128)(2,1)S(1)} %convolution_convert_fusion.2), channel_id=1, replica_groups=mesh['seq'=4,'batch'=8] {'seq'}, dimensions={0}, use_global_device_ids=true | all-gather | bytes 245760 | tf_op jit(solution)/shard_map/all_gather | solution.py:100
  46.1 0.4 convolution_convert_fusion.1
  46.4 6.6 %all_gather.25 = bf16[768,192]{1,0:T(8,128)(2,1)S(1)} all-gather(bf16[192,192]{1,0:T(8,128)(2,1)S(1)} %convolution_convert_fusion.1), channel_id=1, replica_groups=mesh['seq'=4,'batch'=8] {'seq'}, dimensions={0}, use_global_device_ids=true | all-gather | bytes 368640 | tf_op jit(solution)/shard_map/all_gather | solution.py:101
  53.1 3.1 %convolution_convert_fusion = bf16[192,1024]{1,0:T(8,128)(2,1)S(1)} fusion(bf16[1536,1024]{1,0:T(8,128)(2,1)} %all-gather.4.cloned.1.call-done, bf16[192,1536]{1,0:T(8,128)(2,1)S(1)} %get-tuple-element.29, f32[1536]{0:T(1024)S(1)} %copy-done.14, f32[192]{0:T(256)S(1)} %add_rsqrt_fusion), kind=kOutput, calls=%fused_computation.15 | convolution fusion | flops 605356032 | bytes 4135680 | tf_op jit(solution)/shard_map/dot_general | solution.py:89
  56.3 0.8 multiply_reduce_fusion
  57.1 0.8 fusion
  57.9 1.1 %fusion.3 = bf16[1536,192]{0,1:T(8,128)(2,1)S(1)} fusion(bf16[768,192]{1,0:T(8,128)(2,1)S(1)} %all_gather.25, f32[768,1536]{1,0:T(8,128)S(1)} %get-tuple-element.37, f32[1536]{0:T(1024)S(1)} %broadcast_maximum_fusion, f32[1536]{0:T(1024)S(1)} %get-tuple-element.33, f32[1536]{0:T(1024)S(1)} %get-tuple-element.32), kind=kOutput, calls=%fused_computation.8 | convolution fusion | flops 457408512 | bytes 5621760 | tf_op jit(solution)/shard_map/while/body/eval_jaxpr/dot_general | solution.py:120
  59.3 0.7 convert_element_type.77
  60.0 24.7 %all-gather.6.cloned.1.call-done = bf16[1536,1536]{1,0:T(8,128)(2,1)} async-done(((bf16[384,1536]{1,0:T(8,128)(2,1)}), bf16[1536,1536]{1,0:T(8,128)(2,1)}) %all-gather.6.cloned.1.call-update) | async-done | bytes 4718608 | tf_op jit(solution)/shard_map/all_gather | solution.py:135
  84.7 3.4 %fusion.4 = bf16[192,1536]{1,0:T(8,128)(2,1)S(1)} fusion(bf16[192,1536]{1,0:T(8,128)(2,1)S(1)} %convert_element_type.77, bf16[1536,1536]{1,0:T(8,128)(2,1)} %all-gather.6.cloned.1.call-done, bf16[192,1536]{1,0:T(8,128)(2,1)S(1)} %get-tuple-element.29), kind=kOutput, calls=%fused_computation.9 | convolution fusion | flops 906854400 | bytes 6488064 | tf_op jit(solution)/shard_map/dot_general | solution.py:133
  88.4 5.6 %all-gather = bf16[4,12,1536]{2,1,0:T(8,128)(2,1)S(1)} all-gather(bf16[1,12,1536]{2,1,0:T(8,128)(2,1)S(1)} %fusion.28), channel_id=1, replica_groups=mesh['seq'=4,'batch'=8] {'seq'}, dimensions={0}, use_global_device_ids=true | all-gather | bytes 184320 | tf_op jit(solution)/shard_map/all_gather | solution.py:144
  94.3 0.8 fusion.25
  (49 shorter events, 1.5 us)
Async XLA Ops:
  7.2 86.9 %copy-start = (bf16[1536,256]{1,0:T(8,128)(2,1)S(1)}, bf16[1536,256]{1,0:T(8,128)(2,1)}, u32[]{:S(2)}) copy-start(bf16[1536,256]{1,0:T(8,128)(2,1)} %param.22) | copy-start | bytes 2359300
  7.2 1.5 %copy-start.4 = (s32[192,128]{1,0:T(8,128)S(1)}, s32[192,128]{1,0:T(8,128)}, u32[]{:S(2)}) copy-start(s32[192,128]{1,0:T(8,128)} %param.13) | copy-start | bytes 294916
  7.2 1.7 %copy-start.1 = (bf16[192,1536]{1,0:T(8,128)(2,1)S(1)}, bf16[192,1536]{1,0:T(8,128)(2,1)}, u32[]{:S(2)}) copy-start(bf16[192,1536]{1,0:T(8,128)(2,1)} %param.12) | copy-start | bytes 1769476
  7.2 1.7 %copy-start.9 = (f32[4,1536]{1,0:T(4,128)S(1)}, f32[4,1536]{1,0:T(4,128)}, u32[]{:S(2)}) copy-start(f32[4,1536]{1,0:T(4,128)} %param.14) | copy-start | bytes 73732
  7.2 45.9 %all-gather.4.cloned.1.call-start = ((), (), s32[]{:S(2)}) async-start(), calls=%async_computation | async-start | bytes 3932160 | tf_op jit(solution)/shard_map/all_gather | solution.py:83
  7.9 76.8 %all-gather.6.cloned.1.call-start = ((), (), s32[]{:S(2)}) async-start(), calls=%async_computation.1 | async-start | bytes 5898240 | tf_op jit(solution)/shard_map/all_gather | solution.py:135
  8.7 1.5 %copy-start.11 = (f32[1536]{0:T(1024)S(1)}, f32[1536]{0:T(1024)}, u32[]{:S(2)}) copy-start(f32[1536]{0:T(1024)} %param.15) | copy-start | bytes 18436
  10.2 5.1 %copy-start.5 = (bf16[384,128]{1,0:T(8,128)(2,1)S(1)}, bf16[384,128]{1,0:T(8,128)(2,1)}, u32[]{:S(2)}) copy-start(bf16[384,128]{1,0:T(8,128)(2,1)} %param.19) | copy-start | bytes 294916
  10.3 15.9 %copy-start.3 = (bf16[384,192]{0,1:T(8,128)(2,1)S(1)}, bf16[384,192]{0,1:T(8,128)(2,1)}, u32[]{:S(2)}) copy-start(bf16[384,192]{0,1:T(8,128)(2,1)} %param.20) | copy-start | bytes 442372
  10.3 27.0 %copy-start.10 = (f32[5,1536]{1,0:T(8,128)S(1)}, f32[5,1536]{1,0:T(8,128)}, u32[]{:S(2)}) copy-start(f32[5,1536]{1,0:T(8,128)} %param.16) | copy-start | bytes 92164
  11.1 26.9 %collective-permute-start = (bf16[8,1536]{1,0:T(8,128)(2,1)}, bf16[8,1536]{1,0:T(8,128)(2,1)}, u32[]{:S(2)}, u32[]{:S(2)}) collective-permute-start(bf16[8,1536]{1,0:T(8,128)(2,1)} %get-tuple-element.30), channel_id=1, source_target_pairs={{0,8},{8,16},{16,24},{1,9},{9,17},{17,25},{2,10},{10,18},{18,26},{... | collective-permute-start | bytes 73736 | tf_op jit(solution)/shard_map/ppermute | solution.py:25
  14.0 24.0 %collective-permute-start.1 = (bf16[8,1536]{1,0:T(8,128)(2,1)}, bf16[8,1536]{1,0:T(8,128)(2,1)}, u32[]{:S(2)}, u32[]{:S(2)}) collective-permute-start(bf16[8,1536]{1,0:T(8,128)(2,1)} %get-tuple-element.31), channel_id=1, source_target_pairs={{8,0},{16,8},{24,16},{9,1},{17,9},{25,17},{10,2},{18,10},{26,18},{... | collective-permute-start | bytes 73736 | tf_op jit(solution)/shard_map/ppermute | solution.py:27
  38.0 0.9 copy-start.6
  38.0 1.0 copy-start.7
  38.0 1.0 copy-start.8
  39.0 1.1 %copy-start.13 = (f32[1536]{0:T(1024)S(1)}, f32[1536]{0:T(1024)}, u32[]{:S(2)}) copy-start(f32[1536]{0:T(1024)} %param.17) | copy-start | bytes 18436
  46.1 7.0 %copy-start.14 = (f32[1536]{0:T(1024)S(1)}, f32[1536]{0:T(1024)}, u32[]{:S(2)}) copy-start(f32[1536]{0:T(1024)} %param.17) | copy-start | bytes 18436
  88.1 6.2 %copy-start.2 = (bf16[192,1536]{1,0:T(8,128)(2,1)}, bf16[192,1536]{1,0:T(8,128)(2,1)S(1)}, u32[]{:S(2)}) copy-start(bf16[192,1536]{1,0:T(8,128)(2,1)S(1)} %fusion.4) | copy-start | bytes 1769476
  88.1 6.2 %copy-start.12 = (bf16[128,128]{1,0:T(8,128)(2,1)S(1)}, bf16[128,128]{1,0:T(8,128)(2,1)}, u32[]{:S(2)}) copy-start(bf16[128,128]{1,0:T(8,128)(2,1)} %param.23) | copy-start | bytes 98308
Sparse Core Ops, SparseCore 0:
  9.6 35.6 all-gather.3
  46.9 37.7 all-gather.5
where the time goes:
time: 102 us
  blocking collectives  39.8 us (39%)
  waiting for transfers between devices  26.1 us (26%)
  between operations  14.4 us (14%)
  matrix products  11.5 us (11%)
  starting transfers between devices  4.3 us (4%)
  other arithmetic  3.4 us (3%)
  local copies, waits for them, and re-layouts  2.53 us (2%)
    all_gather x1, waiting for transfers between devices, local(): lax.all_gather(out_weight, 'seq', axis=0, tiled=True)  24.7 us
    all_gather x1, blocking collectives, local(): lax.all_gather(value_weight, 'seq', axis=0, tiled=True)  11.2 us
    all_gather x1, blocking collectives, local(): lax.all_gather(key_weight, 'seq', axis=0, tiled=True)  10.8 us
    all_gather x1, blocking collectives, local(): value_piece = lax.all_gather(values_local, 'seq', axis=0, tiled=True)  6.62 us
    all_gather x1, blocking collectives, local(): all_pooled = lax.all_gather(pooled, 'seq', axis=0, tiled=True)  5.61 us
    all_gather x1, blocking collectives, local(): key_piece = lax.all_gather(keys_local, 'seq', axis=0, tiled=True)  5.61 us
    dot_general x3, matrix products, local(): jnp.dot(columns, piece, preferred_element_type=jnp.float32)  3.81 us
    dot_general x1, matrix products, local(): jnp.dot(columns, lax.all_gather(out_weight, 'seq', axis=0, tiled=True), p...  3.42 us
  transfers between devices with their start and end apart: 4, of which 1 were waited for; matrix products, arithmetic and copies ran while one was open for 12% of the time, Pallas kernels for 0%

commit v1 on v0

v1 whole, which is shorter than its diff:
```python
import functools
import math

import jax
import jax.numpy as jnp
from jax import lax
from jax.experimental import pallas as pl
from jax.experimental.pallas import tpu as pltpu
from jax.sharding import PartitionSpec as P

H = 8
DK = 128
DV = 192
BASES = 128
POOL = 16
KERNEL_TAPS = 5
DILATION_STEP = 4
REACH = DILATION_STEP * (KERNEL_TAPS - 1) // 2
EDGE = 16
PAIRS = H // 2
F32 = jnp.float32
BF16 = jnp.bfloat16


def cut(rows, most):
    parts = most
    while rows % parts or (rows // parts) % 16:
        parts -= 1
    return parts


def kernel(
    n,
    tower,
    dna,
    dna_weight,
    conv_gain,
    taps,
    attn_gain,
    query_hbm,
    key_hbm,
    value_hbm,
    out_hbm,
    pair_in_hbm,
    pair_hbm,
    out_ref,
    pair_ref,
    wk,
    wv,
    wq,
    wo,
    pair_in,
    pair_w,
    stream_s,
    padded,
    edges,
    halo,
    conv_s,
    attn_s,
    q_s,
    k_all,
    v_all,
    ctx_s,
    pooled_s,
    left_s,
    slots,
    right_s,
    outer_s,
    halo_sem,
    local_sem,
    own_sem,
    y_send,
    y_recv,
    x_send,
    x_recv,
    f_send,
    f_recv,
    g_send,
    g_recv,
    kv_send,
    kv_recv,
    r_send,
    r_recv,
):
    rows, channels = tower.shape
    seq = lax.axis_index("seq")
    batch = lax.axis_index("batch")
    chips = n // 2
    y, core = seq // 2, lax.rem(seq, 2)
    parity = lax.rem(batch, 2)
    x_other = batch + 1 - 2 * parity
    c_other = seq + 1 - 2 * core

    def at(s, b):
        return {"seq": s, "batch": b}

    hbm = (key_hbm, value_hbm, query_hbm, out_hbm)
    full = (wk, wv, wq, wo)
    block = query_hbm.shape[0]
    half = block // 2
    q_parts, o_parts = cut(half, 2), cut(half, PAIRS)
    q_len, o_len = half // q_parts, half // o_parts
    q_first, o_first = 2, 2 + q_parts

    def span(owner, side, offset, length):
        return pl.ds(pl.multiple_of(owner * block + side * half + offset, 16), length)

    def piece(index):
        if not isinstance(index, int):
            return 3, (index - o_first) * o_len, o_len
        if index < 2:
            return index, 0, half
        if index < o_first:
            return 2, (index - q_first) * q_len, q_len
        return 3, (index - o_first) * o_len, o_len

    def remote(src, dst, send, recv, where):
        return pltpu.make_async_remote_copy(
            src_ref=src,
            dst_ref=dst,
            send_sem=send,
            recv_sem=recv,
            device_id=where,
            device_id_type=pl.DeviceIdType.MESH,
        )

    def held(index, owner, side):
        which, offset, length = piece(index)
        return full[which].at[span(owner, side, offset, length), :]

    def y_copy(j, index):
        which, offset, length = piece(index)
        src = hbm[which].at[pl.ds(pl.multiple_of(parity * half + offset, 16), length), :]
        to = lax.rem(y + j, chips) * 2 + core
        return remote(src, held(index, seq, parity), y_send.at[j - 1, index], y_recv.at[j - 1, index], at(to, batch))

    def source(j):
        return lax.rem(y + chips - j, chips) * 2

    def y_arrived(j, index):
        ref = held(index, source(j) + core, parity)
        return remote(ref, ref, y_send.at[j - 1, index], y_recv.at[j - 1, index], at(seq, batch))

    def x_copy(j, index, side):
        ref = held(index, source(j) + core, side)
        return remote(ref, ref, x_send.at[j - 1, index], x_recv.at[j - 1, index], at(seq, x_other))

    def f_copy(j, index, who):
        ref = held(index, source(j) + who, parity)
        return remote(ref, ref, f_send.at[j - 1, index], f_recv.at[j - 1, index], at(c_other, batch))

    def g_copy(j, index, who):
        ref = held(index, source(j) + who, 1 - parity)
        return remote(ref, ref, g_send.at[j - 1, index], g_recv.at[j - 1, index], at(c_other, batch))

    def own_copy(which, owner):
        ref = full[which].at[pl.ds(pl.multiple_of(owner * block, 16), block), :]
        return remote(hbm[which], ref, own_sem.at[0, which], own_sem.at[1, which], at(c_other, batch))

    def local_copy(which):
        ref = full[which].at[pl.ds(pl.multiple_of(seq * block, 16), block), :]
        return pltpu.make_async_copy(hbm[which], ref, local_sem.at[which])

    def from_y(index):
        for j in range(1, chips):
            y_arrived(j, index).wait_recv()
            x_copy(j, index, parity).start()
            f_copy(j, index, core).start()

    def from_x(index):
        for j in range(1, chips):
            x_copy(j, index, 1 - parity).wait_recv()
            g_copy(j, index, core).start()

    def from_core(index):
        for j in range(1, chips):
            f_copy(j, index, 1 - core).wait_recv()
            g_copy(j, index, 1 - core).wait_recv()

    barrier = pltpu.get_barrier_semaphore()
    for k in range(1, n):
        pl.semaphore_signal(
            barrier, inc=1, device_id=at(lax.rem(seq + k, n), batch), device_id_type=pl.DeviceIdType.MESH
        )
    pl.semaphore_signal(barrier, inc=1, device_id=at(seq, x_other), device_id_type=pl.DeviceIdType.MESH)
    for which in range(4):
        local_copy(which).start()
    pair_in_copy = pltpu.make_async_copy(pair_in_hbm, pair_in, local_sem.at[4])
    pair_copy = pltpu.make_async_copy(pair_hbm, pair_w, local_sem.at[5])
    pair_in_copy.start()
    pair_copy.start()

    def normalise(first, count, width):
        rows_at = pl.ds(first, count)
        bases = dna[rows_at, :]
        shares = [
            (jnp.sum((bases == b).astype(F32), axis=1, keepdims=True) - BASES / 4.0)
            * (4.0 / math.sqrt(3.0 * BASES))
            for b in range(4)
        ]

        def add(i, total):
            cols = pl.ds(pl.multiple_of(i * width, 128), width)
            value = tower[rows_at, cols].astype(F32)
            for b in range(4):
                value = value + shares[b] * dna_weight[pl.ds(b, 1), cols]
            stream_s[rows_at, cols] = value
            square = value * value
            for g in range(width // 128):
                total = total + square[:, g * 128 : (g + 1) * 128]
            return total

        total = lax.fori_loop(0, channels // width, add, jnp.zeros((count, 128), F32))
        factor = lax.rsqrt(jnp.sum(total, axis=1, keepdims=True) * (1.0 / channels) + 1e-6)

        def scale(i, carry):
            cols = pl.ds(pl.multiple_of(i * width, 128), width)
            value = (stream_s[rows_at, cols] * factor * conv_gain[:, cols]).astype(BF16)
            padded[pl.ds(REACH + first, count), cols] = value.astype(F32)
            if first == 0:
                edges[0, :, cols] = value
            elif first == rows - EDGE:
                edges[1, :, cols] = value
            return carry

        lax.fori_loop(0, channels // width, scale, 0)

    normalise(0, EDGE, channels)
    normalise(rows - EDGE, EDGE, channels)

    pl.semaphore_wait(barrier, n)

    to_left = remote(edges.at[0], halo.at[1], halo_sem.at[0], halo_sem.at[1], at(jnp.maximum(seq - 1, 0), batch))
    to_right = remote(edges.at[1], halo.at[0], halo_sem.at[2], halo_sem.at[3], at(jnp.minimum(seq + 1, n - 1), batch))

    @pl.when(seq > 0)
    def _():
        to_left.start()

    @pl.when(seq < n - 1)
    def _():
        to_right.start()

    for index in range(o_first):
        for j in range(1, chips):
            y_copy(j, index).start()
    for which in range(3):
        own_copy(which, seq).start()
    for index in range(o_first, o_first + o_parts):
        for j in range(1, chips):
            y_copy(j, index).start()

    normalise(EDGE, rows - 2 * EDGE, 128)
    from_y(0)
    from_y(1)

    @pl.when(seq > 0)
    def _():
        to_right.wait_recv()
        padded[pl.ds(0, REACH), :] = halo[0].astype(F32)[EDGE - REACH :]

    @pl.when(seq == 0)
    def _():
        padded[pl.ds(0, REACH), :] = jnp.zeros((REACH, channels), F32)

    @pl.when(seq < n - 1)
    def _():
        to_left.wait_recv()
        padded[pl.ds(REACH + rows, REACH), :] = halo[1].astype(F32)[:REACH]

    @pl.when(seq == n - 1)
    def _():
        padded[pl.ds(REACH + rows, REACH), :] = jnp.zeros((REACH, channels), F32)

    def convolve(i, total):
        cols = pl.ds(pl.multiple_of(i * 128, 128), 128)
        value = jnp.zeros((rows, 128), F32)
        for t in range(KERNEL_TAPS):
            value = value + taps[pl.ds(t, 1), cols] * padded[pl.ds(t * DILATION_STEP, rows), cols]
        inner = math.sqrt(2.0 / math.pi) * (value + 0.044715 * (value * value * value))
        value = (stream_s[:, cols] + value * (0.5 + 0.5 * jnp.tanh(inner))).astype(BF16)
        conv_s[:, cols] = value
        value = value.astype(F32)
        return total + value * value

    total = lax.fori_loop(0, channels // 128, convolve, jnp.zeros((rows, 128), F32))
    factor = lax.rsqrt(jnp.sum(total, axis=1, keepdims=True) * (1.0 / channels) + 1e-6)

    def renormalise(i, carry):
        cols = pl.ds(pl.multiple_of(i * 128, 128), 128)
        attn_s[:, cols] = (conv_s[:, cols].astype(F32) * factor * attn_gain[:, cols]).astype(BF16)
        return carry

    lax.fori_loop(0, channels // 128, renormalise, 0)

    from_x(0)
    from_x(1)
    from_y(2)
    for which in range(2):
        local_copy(which).wait()
        own_copy(which, c_other).wait_recv()
        from_core(which)
    mine = pl.ds(pl.multiple_of(seq * rows, 16), rows)
    attn_in = attn_s[...]
    k_all[mine, :] = jnp.dot(attn_in, wk[...], preferred_element_type=F32).astype(BF16)
    v_all[mine, :] = jnp.dot(attn_in, wv[...], preferred_element_type=F32).astype(BF16)

    def kv_copy(k, which, owner):
        ref = (k_all, v_all)[which].at[pl.ds(pl.multiple_of(owner * rows, 16), rows), :]
        return remote(ref, ref, kv_send.at[k - 1, which], kv_recv.at[k - 1, which], at(lax.rem(seq + k, n), batch))

    for k in range(1, n):
        for which in range(2):
            kv_copy(k, which, seq).start()
    own_copy(3, seq).start()

    for index in range(3, o_first):
        from_y(index)
    for index in range(2, o_first):
        from_x(index)
    local_copy(2).wait()
    own_copy(2, c_other).wait_recv()
    for index in range(2, o_first):
        from_core(index)

    def query(p, carry):
        cols = pl.ds(pl.multiple_of(p * 2 * DK, 2 * DK), 2 * DK)
        value = jnp.dot(attn_s[...], wq[:, cols], preferred_element_type=F32).astype(BF16)
        q_s[p, pl.ds(0, rows), :] = value[:, :DK]
        q_s[p, pl.ds(rows, rows), :] = value[:, DK:]
        return carry

    lax.fori_loop(0, PAIRS, query, 0)
    for k in range(1, n):
        owner = lax.rem(seq + n - k, n)
        for which in range(2):
            kv_copy(k, which, owner).wait_recv()

    to_power = math.log2(math.e) / math.sqrt(DK)

    def attend(p, carry):
        scores = lax.dot_general(
            q_s[p], k_all[...], (((1,), (1,)), ((), ())), preferred_element_type=F32
        )
        top = jnp.max(scores, axis=1, keepdims=True)
        expo = jnp.exp2((scores - top) * to_power)
        sums = jnp.sum(expo, axis=1, keepdims=True)
        value = jnp.dot(expo.astype(BF16), v_all[...], preferred_element_type=F32)
        value = (value / sums).astype(BF16)
        ctx_s[p, :, pl.ds(0, DV)] = value[:rows]
        ctx_s[p, :, pl.ds(DV, DV)] = value[rows:]
        if o_parts == PAIRS:
            from_y(o_first + p)
        return carry

    lax.fori_loop(0, PAIRS, attend, 0)
    for index in range(o_first, o_first + o_parts):
        if o_parts != PAIRS:
            from_y(index)
        from_x(index)
    local_copy(3).wait()
    own_copy(3, c_other).wait_recv()
    for index in range(o_first, o_first + o_parts):
        from_core(index)

    own_rows = rows // POOL
    pooled_s[...] = jnp.zeros_like(pooled_s)
    width = 512

    def project(i, carry):
        cols = pl.ds(pl.multiple_of(i * width, width), width)
        value = conv_s[:, cols].astype(F32)
        total = jnp.zeros((rows, width), F32)
        for p in range(PAIRS):
            total = total + jnp.dot(
                ctx_s[p], wo[pl.ds(p * 2 * DV, 2 * DV), cols], preferred_element_type=F32
            )
        value = (value + total).astype(BF16)
        out_ref[:, cols] = value
        value = value.astype(F32).reshape(own_rows, POOL, width)
        pooled_s[pl.ds(0, own_rows), cols] = jnp.sum(value, axis=1) * (1.0 / POOL)
        return carry

    lax.fori_loop(0, channels // width, project, 0)
    pair_in_copy.wait()
    pair_copy.wait()
    features = jnp.dot(pooled_s[...].astype(BF16), pair_in[...], preferred_element_type=F32).astype(BF16)
    pair_width = pair_w.shape[0]
    left_s[...] = features[:, :pair_width].astype(F32)
    slots[seq] = features[:, pair_width:]

    def r_copy(k, owner):
        ref = slots.at[owner]
        return remote(ref, ref, r_send.at[k - 1], r_recv.at[k - 1], at(lax.rem(seq + k, n), batch))

    for k in range(1, n):
        r_copy(k, seq).start()
    for index in range(o_first + o_parts):
        for j in range(1, chips):
            y_copy(j, index).wait_send()
            x_copy(j, index, parity).wait_send()
            f_copy(j, index, core).wait_send()
            g_copy(j, index, core).wait_send()
    for which in range(4):
        own_copy(which, seq).wait_send()
    for k in range(1, n):
        for which in range(2):
            kv_copy(k, which, seq).wait_send()

    @pl.when(seq > 0)
    def _():
        to_left.wait_send()

    @pl.when(seq < n - 1)
    def _():
        to_right.wait_send()

    for k in range(1, n):
        r_copy(k, lax.rem(seq + n - k, n)).wait_recv()
    for owner in range(n):
        right_s[pl.ds(owner * own_rows, own_rows), :] = slots[owner].astype(F32)[:own_rows]
    all_rows = n * own_rows
    for i in range(own_rows):
        outer_s[pl.ds(i * all_rows, all_rows), :] = (left_s[pl.ds(i, 1), :] * right_s[...]).astype(BF16)
    mixed = jnp.dot(outer_s[...], pair_w[...], preferred_element_type=F32)
    for i in range(own_rows):
        pair_ref[i] = (
            mixed[i * all_rows : (i + 1) * all_rows] + left_s[pl.ds(i, 1), :] + right_s[...]
        ).astype(BF16)
    for k in range(1, n):
        r_copy(k, seq).wait_send()


def local(
    n,
    tower,
    dna,
    dna_weight,
    conv_gain,
    depthwise_kernel,
    attn_gain,
    query_weight,
    key_weight,
    value_weight,
    out_weight,
    pair_in_weight,
    pair_weight,
):
    rows, channels = tower.shape
    block = query_weight.shape[0]
    depth = n * block
    chips = n // 2
    pair_width = pair_weight.shape[0]
    own_rows = rows // POOL
    all_rows = n * own_rows
    pieces = 2 + cut(block // 2, 2) + cut(block // 2, PAIRS)
    dma = pltpu.SemaphoreType.DMA
    vmem = pl.BlockSpec(memory_space=pltpu.VMEM)
    anywhere = pl.BlockSpec(memory_space=pl.ANY)
    return pl.pallas_call(
        functools.partial(kernel, n),
        out_shape=(
            jax.ShapeDtypeStruct((rows, channels), BF16),
            jax.ShapeDtypeStruct((own_rows, all_rows, pair_width), BF16),
        ),
        in_specs=[vmem] * 6 + [anywhere] * 6,
        out_specs=(vmem, vmem),
        scratch_shapes=[
            pltpu.VMEM((depth, DK), BF16),
            pltpu.VMEM((depth, DV), BF16),
            pltpu.VMEM((depth, H * DK), BF16),
            pltpu.VMEM((depth, out_weight.shape[1]), BF16),
            pltpu.VMEM(pair_in_weight.shape, BF16),
            pltpu.VMEM(pair_weight.shape, BF16),
            pltpu.VMEM((rows, channels), F32),
            pltpu.VMEM((rows + 2 * REACH, channels), F32),
            pltpu.VMEM((2, EDGE, channels), BF16),
            pltpu.VMEM((2, EDGE, channels), BF16),
            pltpu.VMEM((rows, channels), BF16),
            pltpu.VMEM((rows, channels), BF16),
            pltpu.VMEM((PAIRS, 2 * rows, DK), BF16),
            pltpu.VMEM((n * rows, DK), BF16),
            pltpu.VMEM((n * rows, DV), BF16),
            pltpu.VMEM((PAIRS, rows, 2 * DV), BF16),
            pltpu.VMEM((16, channels), F32),
            pltpu.VMEM((16, pair_width), F32),
            pltpu.VMEM((n, 16, pair_width), BF16),
            pltpu.VMEM((all_rows, pair_width), F32),
            pltpu.VMEM((own_rows * all_rows, pair_width), BF16),
            dma((4,)),
            dma((6,)),
            dma((2, 4)),
        ]
        + [dma((chips - 1, pieces))] * 8
        + [dma((n - 1, 2))] * 2
        + [dma((n - 1,))] * 2,
        compiler_params=pltpu.CompilerParams(
            collective_id=0, has_side_effects=True, vmem_limit_bytes=56 * 1024 * 1024
        ),
    )(
        tower,
        dna,
        dna_weight,
        conv_gain.reshape(1, channels),
        depthwise_kernel,
        attn_gain.reshape(1, channels),
        query_weight,
        key_weight,
        value_weight,
        out_weight,
        pair_in_weight,
        pair_weight,
    )


def solution(mesh):
    rows = P(("batch", "seq"), None)
    in_specs = (rows, rows, P(), P(), P(), P()) + (P("seq", None),) * 4 + (P(), P())
    out_specs = (rows, P(("batch", "seq"), None, None))
    return jax.shard_map(
        functools.partial(local, mesh.shape["seq"]),
        mesh=mesh,
        in_specs=in_specs,
        out_specs=out_specs,
        check_vma=False,
    )
```

time: 102 us -> 66.1 us (0.65)
  Pallas kernels: 0 us -> 58.2 us
  blocking collectives: 39.8 us -> 0 us
  waiting for transfers between devices: 26.1 us -> 0 us
  between operations: 14.4 us -> 0.65 us
  matrix products: 11.5 us -> 0 us
  local copies, waits for them, and re-layouts: 2.53 us -> 6.93 us
  starting transfers between devices: 4.3 us -> 0 us
  other arithmetic: 3.4 us -> 0 us
    pallas_call x0 -> x1, Pallas kernels: none -> 58.2 us  [local(): pl.pallas_call(functools.partial(kernel, n), out_shape=(jax.ShapeDtypeStr...]
    all_gather x5 -> x0, blocking collectives: 39.8 us -> none  [the longest x1 11.2 us: local(): lax.all_gather(value_weight, 'seq', axis=0, tiled=True)]
    all_gather x2 -> x0, waiting for transfers between devices: 24.7 us -> none  [the longest x1 24.7 us: local(): lax.all_gather(out_weight, 'seq', axis=0, tiled=True)]
    dot_general x9 -> x0, matrix products: 11.5 us -> none  [the longest x3 3.81 us: local(): jnp.dot(columns, piece, preferred_element_type=jnp.float32)]
    unnamed x31 -> x5, local copies, waits for them, and re-layouts: 0.11 us -> 4.34 us
    ppermute x2 -> x0, starting transfers between devices: 4.22 us -> none  [the longest x1 2.94 us: extended(): lax.ppermute(tail, axis, [(i, (i + 1) % count) for i in range(ends)])]
    reshape x1 -> x2, local copies, waits for them, and re-layouts: 0.17 us -> 2.59 us  [the longest x1 1.3 us: local(): attn_gain.reshape(1, channels)]
    reduce_sum x4 -> x0, other arithmetic: 2.26 us -> none  [the longest x1 1.1 us: rms_norm(): jnp.mean(wide * wide, axis=-1, keepdims=True) + 1e-06]
  transfers between devices with their start and end apart: 4 -> 0, of which waited for: 1 -> 0; matrix products, arithmetic and copies ran while one was open for 12% -> 0% of each run, Pallas kernels for 0% -> 0%
where the time goes in v1:
time: 66.1 us; the launch traced here: 65.8 us
  Pallas kernels  58.2 us (88%)
  local copies, waits for them, and re-layouts  6.93 us (10%)
    pallas_call x1, Pallas kernels, local(): pl.pallas_call(functools.partial(kernel, n), out_shape=(jax.ShapeDtypeStr...  58.2 us
    unnamed x5, local copies, waits for them, and re-layouts  4.34 us

profile of v1, /device:TPU:0, one launch (start us, length us, event | category | flops | bytes accessed | tf_op | source)
XLA Modules:
  0.0 65.8 jit_solution(12736975633011041661)
XLA Ops:
  0.6 1.3 %reshape.10.conv_gain = f32[1,1536]{1,0:T(1,128)} reshape(f32[1536]{0:T(1024)} %param.15) | data formatting | bytes 12288 | tf_op jit(solution)/shard_map/reshape | solution.py:504
  1.9 1.3 %reshape.11.attn_gain = f32[1,1536]{1,0:T(1,128)} reshape(f32[1536]{0:T(1024)} %param.17) | data formatting | bytes 12288 | tf_op jit(solution)/shard_map/reshape | solution.py:506
  3.2 1.7 %copy.14.value_hbm = bf16[384,192]{1,0:T(8,128)(2,1)} copy(bf16[384,192]{0,1:T(8,128)(2,1)} %param.20) | data formatting | bytes 294912 | tf_op args[8]
  4.9 58.2 %shard_map.131 = (bf16[192,1536]{1,0:T(8,128)(2,1)}, bf16[12,48,128]{2,1,0:T(8,128)(2,1)}) custom-call(bf16[192,1536]{1,0:T(8,128)(2,1)} %tower.1, s32[192,128]{1,0:T(8,128)} %dna.1, f32[4,1536]{1,0:T(4,128)} %dna_weight.1, f32[1,1536]{1,0:T(1,128)} %reshape.10.conv_gain, f32[5,1536]{1,0:T(8,128)} %taps.1, f32[1,1536]{1,0:T(1,128)} %reshape.11.attn_gain, ...), custom_call_target="tpu_custom_call" | custom-call | tf_op jit(solution)/shard_map/pallas_call | solution.py:460
  63.2 0.0 copy-start
  63.2 2.0 %copy.17 = bf16[192,1536]{1,0:T(8,128)(2,1)} copy(bf16[192,1536]{1,0:T(8,128)(2,1)} %get-tuple-element.4) | data formatting | bytes 1179648
  65.2 0.0 copy-done
  65.2 0.7 %copy.18 = bf16[12,48,128]{2,1,0:T(8,128)(2,1)} copy(bf16[12,48,128]{2,1,0:T(8,128)(2,1)S(1)} %copy-done) | data formatting | bytes 294912
Async XLA Ops:
  63.2 2.0 %copy-start = (bf16[12,48,128]{2,1,0:T(8,128)(2,1)S(1)}, bf16[12,48,128]{2,1,0:T(8,128)(2,1)}, u32[]{:S(2)}) copy-start(bf16[12,48,128]{2,1,0:T(8,128)(2,1)} %get-tuple-element.5) | copy-start | bytes 442372

commit v2 on v1

--- a/solution.py
+++ b/solution.py
@@ -22,11 +22,22 @@
 BF16 = jnp.bfloat16
 
 
-def cut(rows, most):
-    parts = most
-    while rows % parts or (rows // parts) % 16:
-        parts -= 1
-    return parts
+Y, X, Z, D = range(4)
+
+
+def group_of(block):
+    return 4 if block % 64 == 0 else 2
+
+
+def pieces_of(block):
+    groups = group_of(block)
+    part = block // groups
+    cuts = 2 if part % 32 == 0 else 1
+    length = part // cuts
+    pieces = [(0, 0, part), (1, 0, DV // groups)]
+    for which in (2, 3):
+        pieces += [(which, i * length, length) for i in range(cuts)]
+    return pieces, 2, 2 + cuts
 
 
 def kernel(
@@ -66,17 +77,12 @@
     slots,
     right_s,
     outer_s,
+    gains,
     halo_sem,
     local_sem,
     own_sem,
-    y_send,
-    y_recv,
-    x_send,
-    x_recv,
-    f_send,
-    f_recv,
-    g_send,
-    g_recv,
+    w_send,
+    w_recv,
     kv_send,
     kv_recv,
     r_send,
@@ -87,32 +93,24 @@
     batch = lax.axis_index("batch")
     chips = n // 2
     y, core = seq // 2, lax.rem(seq, 2)
-    parity = lax.rem(batch, 2)
-    x_other = batch + 1 - 2 * parity
+    by_x = lax.rem(batch, 2)
+    by_z = lax.rem(batch // 2, 2)
     c_other = seq + 1 - 2 * core
 
     def at(s, b):
         return {"seq": s, "batch": b}
 
+    core_peer = at(c_other, batch)
+    x_peer = at(seq, batch + 1 - 2 * by_x)
+    z_peer = at(seq, batch + 2 - 4 * by_z)
     hbm = (key_hbm, value_hbm, query_hbm, out_hbm)
     full = (wk, wv, wq, wo)
     block = query_hbm.shape[0]
-    half = block // 2
-    q_parts, o_parts = cut(half, 2), cut(half, PAIRS)
-    q_len, o_len = half // q_parts, half // o_parts
-    q_first, o_first = 2, 2 + q_parts
-
-    def span(owner, side, offset, length):
-        return pl.ds(pl.multiple_of(owner * block + side * half + offset, 16), length)
-
-    def piece(index):
-        if not isinstance(index, int):
-            return 3, (index - o_first) * o_len, o_len
-        if index < 2:
-            return index, 0, half
-        if index < o_first:
-            return 2, (index - q_first) * q_len, q_len
-        return 3, (index - o_first) * o_len, o_len
+    groups = group_of(block)
+    part = block // groups
+    pieces, first_query, first_out = pieces_of(block)
+    mine = by_x if groups == 2 else 2 * by_z + by_x
+    quarter = {Y: mine, X: mine + 1 - 2 * by_x, Z: mine + 2 - 4 * by_z, D: groups - 1 - mine}
 
     def remote(src, dst, send, recv, where):
         return pltpu.make_async_remote_copy(
@@ -125,64 +123,90 @@
         )
 
     def held(index, owner, side):
-        which, offset, length = piece(index)
-        return full[which].at[span(owner, side, offset, length), :]
-
-    def y_copy(j, index):
-        which, offset, length = piece(index)
-        src = hbm[which].at[pl.ds(pl.multiple_of(parity * half + offset, 16), length), :]
-        to = lax.rem(y + j, chips) * 2 + core
-        return remote(src, held(index, seq, parity), y_send.at[j - 1, index], y_recv.at[j - 1, index], at(to, batch))
+        which, offset, length = pieces[index]
+        if which == 1:
+            return wv.at[owner, pl.ds(pl.multiple_of(side * length, 16), length), :]
+        return full[which].at[pl.ds(pl.multiple_of(owner * block + side * part + offset, 16), length), :]
+
+    def weight_copy(route, j, index, ref, where, src=None):
+        sems = (w_send.at[route, j - 1, index], w_recv.at[route, j - 1, index])
+        return remote(ref if src is None else src, ref, *sems, where)
 
     def source(j):
         return lax.rem(y + chips - j, chips) * 2
 
-    def y_arrived(j, index):
-        ref = held(index, source(j) + core, parity)
-        return remote(ref, ref, y_send.at[j - 1, index], y_recv.at[j - 1, index], at(seq, batch))
-
-    def x_copy(j, index, side):
-        ref = held(index, source(j) + core, side)
-        return remote(ref, ref, x_send.at[j - 1, index], x_recv.at[j - 1, index], at(seq, x_other))
-
-    def f_copy(j, index, who):
-        ref = held(index, source(j) + who, parity)
-        return remote(ref, ref, f_send.at[j - 1, index], f_recv.at[j - 1, index], at(c_other, batch))
-
-    def g_copy(j, index, who):
-        ref = held(index, source(j) + who, 1 - parity)
-        return remote(ref, ref, g_send.at[j - 1, index], g_recv.at[j - 1, index], at(c_other, batch))
+    def y_copy(j, index):
+        which, offset, length = pieces[index]
+        start = mine * (length if which == 1 else part) + offset
+        src = hbm[which].at[pl.ds(pl.multiple_of(start, 16), length), :]
+        to = lax.rem(y + j, chips) * 2 + core
+        return weight_copy(Y, j, index, held(index, seq, mine), at(to, batch), src)
+
+    def arrival(route, j, index):
+        ref = held(index, source(j) + core, quarter[route])
+        return weight_copy(route, j, index, ref, core_peer)
+
+    def x_copy(j, index):
+        return weight_copy(X, j, index, held(index, source(j) + core, mine), x_peer)
+
+    def z_copy(j, index):
+        return weight_copy(Z, j, index, held(index, source(j) + core, mine), z_peer)
+
+    def d_copy(j, index):
+        via, peer = (X, z_peer) if index % 2 == 0 else (Z, x_peer)
+        return weight_copy(D, j, index, held(index, source(j) + core, quarter[via]), peer)
+
+    def c_copy(route, j, index, who):
+        ref = held(index, source(j) + who, quarter[route])
+        return weight_copy(route + 4, j, index, ref, core_peer)
 
     def own_copy(which, owner):
-        ref = full[which].at[pl.ds(pl.multiple_of(owner * block, 16), block), :]
-        return remote(hbm[which], ref, own_sem.at[0, which], own_sem.at[1, which], at(c_other, batch))
+        if which == 1:
+            ref = wv.at[owner]
+        else:
+            ref = full[which].at[pl.ds(pl.multiple_of(owner * block, 16), block), :]
+        return remote(hbm[which], ref, own_sem.at[0, which], own_sem.at[1, which], core_peer)
 
     def local_copy(which):
-        ref = full[which].at[pl.ds(pl.multiple_of(seq * block, 16), block), :]
+        if which == 1:
+            ref = wv.at[seq]
+        else:
+            ref = full[which].at[pl.ds(pl.multiple_of(seq * block, 16), block), :]
         return pltpu.make_async_copy(hbm[which], ref, local_sem.at[which])
 
-    def from_y(index):
+    routes = (Y, X) if groups == 2 else (Y, X, Z, D)
+
+    def forward(route, index):
+        if route not in routes:
+            return
         for j in range(1, chips):
-            y_arrived(j, index).wait_recv()
-            x_copy(j, index, parity).start()
-            f_copy(j, index, core).start()
-
-    def from_x(index):
-        for j in range(1, chips):
-            x_copy(j, index, 1 - parity).wait_recv()
-            g_copy(j, index, core).start()
+            arrival(route, j, index).wait_recv()
+            if route == Y:
+                x_copy(j, index).start()
+                if groups == 4:
+                    z_copy(j, index).start()
+            if groups == 4 and route == (X if index % 2 == 0 else Z):
+                d_copy(j, index).start()
+            c_copy(route, j, index, core).start()
 
     def from_core(index):
         for j in range(1, chips):
-            f_copy(j, index, 1 - core).wait_recv()
-            g_copy(j, index, 1 - core).wait_recv()
+            for route in routes:
+                c_copy(route, j, index, 1 - core).wait_recv()
+
+    q_pieces = range(first_query, first_out)
+    o_pieces = range(first_out, len(pieces))
 
     barrier = pltpu.get_barrier_semaphore()
     for k in range(1, n):
         pl.semaphore_signal(
             barrier, inc=1, device_id=at(lax.rem(seq + k, n), batch), device_id_type=pl.DeviceIdType.MESH
         )
-    pl.semaphore_signal(barrier, inc=1, device_id=at(seq, x_other), device_id_type=pl.DeviceIdType.MESH)
+    pl.semaphore_signal(barrier, inc=1, device_id=x_peer, device_id_type=pl.DeviceIdType.MESH)
+    if groups == 4:
+        pl.semaphore_signal(barrier, inc=1, device_id=z_peer, device_id_type=pl.DeviceIdType.MESH)
+    gains[pl.ds(0, 1), :] = conv_gain[...].reshape(1, channels)
+    gains[pl.ds(1, 1), :] = attn_gain[...].reshape(1, channels)
     for which in range(4):
         local_copy(which).start()
     pair_in_copy = pltpu.make_async_copy(pair_in_hbm, pair_in, local_sem.at[4])
@@ -215,7 +239,7 @@
 
         def scale(i, carry):
             cols = pl.ds(pl.multiple_of(i * width, 128), width)
-            value = (stream_s[rows_at, cols] * factor * conv_gain[:, cols]).astype(BF16)
+            value = (stream_s[rows_at, cols] * factor * gains[pl.ds(0, 1), cols]).astype(BF16)
             padded[pl.ds(REACH + first, count), cols] = value.astype(F32)
             if first == 0:
                 edges[0, :, cols] = value
@@ -228,7 +252,7 @@
     normalise(0, EDGE, channels)
     normalise(rows - EDGE, EDGE, channels)
 
-    pl.semaphore_wait(barrier, n)
+    pl.semaphore_wait(barrier, n if groups == 2 else n + 1)
 
     to_left = remote(edges.at[0], halo.at[1], halo_sem.at[0], halo_sem.at[1], at(jnp.maximum(seq - 1, 0), batch))
     to_right = remote(edges.at[1], halo.at[0], halo_sem.at[2], halo_sem.at[3], at(jnp.minimum(seq + 1, n - 1), batch))
@@ -241,18 +265,18 @@
     def _():
         to_right.start()
 
-    for index in range(o_first):
+    for index in range(first_out):
         for j in range(1, chips):
             y_copy(j, index).start()
     for which in range(3):
         own_copy(which, seq).start()
-    for index in range(o_first, o_first + o_parts):
+    for index in o_pieces:
         for j in range(1, chips):
             y_copy(j, index).start()
 
     normalise(EDGE, rows - 2 * EDGE, 128)
-    from_y(0)
-    from_y(1)
+    for index in range(2):
+        forward(Y, index)
 
     @pl.when(seq > 0)
     def _():
@@ -286,41 +310,70 @@
     total = lax.fori_loop(0, channels // 128, convolve, jnp.zeros((rows, 128), F32))
     factor = lax.rsqrt(jnp.sum(total, axis=1, keepdims=True) * (1.0 / channels) + 1e-6)
 
+    for index in range(2):
+        forward(X, index)
+        forward(Z, index)
+
     def renormalise(i, carry):
         cols = pl.ds(pl.multiple_of(i * 128, 128), 128)
-        attn_s[:, cols] = (conv_s[:, cols].astype(F32) * factor * attn_gain[:, cols]).astype(BF16)
+        attn_s[:, cols] = (conv_s[:, cols].astype(F32) * factor * gains[pl.ds(1, 1), cols]).astype(BF16)
         return carry
 
     lax.fori_loop(0, channels // 128, renormalise, 0)
 
-    from_x(0)
-    from_x(1)
-    from_y(2)
+    for index in q_pieces:
+        forward(Y, index)
+    for index in range(2):
+        forward(D, index)
     for which in range(2):
         local_copy(which).wait()
         own_copy(which, c_other).wait_recv()
         from_core(which)
-    mine = pl.ds(pl.multiple_of(seq * rows, 16), rows)
     attn_in = attn_s[...]
-    k_all[mine, :] = jnp.dot(attn_in, wk[...], preferred_element_type=F32).astype(BF16)
-    v_all[mine, :] = jnp.dot(attn_in, wv[...], preferred_element_type=F32).astype(BF16)
-
-    def kv_copy(k, which, owner):
-        ref = (k_all, v_all)[which].at[pl.ds(pl.multiple_of(owner * rows, 16), rows), :]
-        return remote(ref, ref, kv_send.at[k - 1, which], kv_recv.at[k - 1, which], at(lax.rem(seq + k, n), batch))
-
-    for k in range(1, n):
+
+    def own(owner):
+        return pl.ds(pl.multiple_of(owner * rows, 16), rows)
+
+    k_all[own(seq), :] = jnp.dot(attn_in, wk[...], preferred_element_type=F32).astype(BF16)
+    value = jnp.zeros((rows, DV), F32)
+    for owner in range(n):
+        value = value + lax.dot_general(
+            attn_s[:, pl.ds(owner * block, block)],
+            wv[owner],
+            (((1,), (1,)), ((), ())),
+            preferred_element_type=F32,
+        )
+    v_all[own(seq), :] = value.astype(BF16)
+
+    def kv_copy(slot, which, owner, where):
+        ref = (k_all, v_all)[which].at[own(owner), :]
+        return remote(ref, ref, kv_send.at[slot, which], kv_recv.at[slot, which], where)
+
+    def kv_sends(slot, which):
+        if slot == 0:
+            return kv_copy(0, which, seq, core_peer)
+        if slot < chips:
+            return kv_copy(slot, which, seq, at(lax.rem(y + slot, chips) * 2 + core, batch))
+        return kv_copy(slot, which, source(slot - chips + 1) + core, core_peer)
+
+    for slot in list(range(1, chips)) + [0]:
         for which in range(2):
-            kv_copy(k, which, seq).start()
+            kv_sends(slot, which).start()
+    for index in q_pieces:
+        forward(X, index)
+        forward(Z, index)
     own_copy(3, seq).start()
-
-    for index in range(3, o_first):
-        from_y(index)
-    for index in range(2, o_first):
-        from_x(index)
+    for index in o_pieces:
+        forward(Y, index)
+    for index in q_pieces:
+        forward(D, index)
+    for j in range(1, chips):
+        for which in range(2):
+            kv_copy(j, which, source(j) + core, core_peer).wait_recv()
+            kv_sends(chips - 1 + j, which).start()
     local_copy(2).wait()
     own_copy(2, c_other).wait_recv()
-    for index in range(2, o_first):
+    for index in q_pieces:
         from_core(index)
 
     def query(p, carry):
@@ -331,10 +384,10 @@
         return carry
 
     lax.fori_loop(0, PAIRS, query, 0)
-    for k in range(1, n):
-        owner = lax.rem(seq + n - k, n)
-        for which in range(2):
-            kv_copy(k, which, owner).wait_recv()
+    for which in range(2):
+        kv_copy(0, which, c_other, core_peer).wait_recv()
+        for j in range(1, chips):
+            kv_copy(chips - 1 + j, which, source(j) + 1 - core, core_peer).wait_recv()
 
     to_power = math.log2(math.e) / math.sqrt(DK)
 
@@ -349,18 +402,24 @@
         value = (value / sums).astype(BF16)
         ctx_s[p, :, pl.ds(0, DV)] = value[:rows]
         ctx_s[p, :, pl.ds(DV, DV)] = value[rows:]
-        if o_parts == PAIRS:
-            from_y(o_first + p)
+
+        for index in o_pieces:
+
+            @pl.when(p == index - first_out)
+            def _():
+                forward(X, index)
+                forward(Z, index)
+
+            @pl.when(p == index - first_out + 2)
+            def _():
+                forward(D, index)
+
         return carry
 
     lax.fori_loop(0, PAIRS, attend, 0)
-    for index in range(o_first, o_first + o_parts):
-        if o_parts != PAIRS:
-            from_y(index)
-        from_x(index)
     local_copy(3).wait()
     own_copy(3, c_other).wait_recv()
-    for index in range(o_first, o_first + o_parts):
+    for index in o_pieces:
         from_core(index)
 
     own_rows = rows // POOL
@@ -395,17 +454,20 @@
 
     for k in range(1, n):
         r_copy(k, seq).start()
-    for index in range(o_first + o_parts):
+    for index in range(len(pieces)):
         for j in range(1, chips):
             y_copy(j, index).wait_send()
-            x_copy(j, index, parity).wait_send()
-            f_copy(j, index, core).wait_send()
-            g_copy(j, index, core).wait_send()
+            x_copy(j, index).wait_send()
+            if groups == 4:
+                z_copy(j, index).wait_send()
+                d_copy(j, index).wait_send()
+            for route in routes:
+                c_copy(route, j, index, core).wait_send()
     for which in range(4):
         own_copy(which, seq).wait_send()
-    for k in range(1, n):
+    for slot in range(2 * chips - 1):
         for which in range(2):
-            kv_copy(k, which, seq).wait_send()
+            kv_sends(slot, which).wait_send()
 
     @pl.when(seq > 0)
     def _():
@@ -453,7 +515,7 @@
     pair_width = pair_weight.shape[0]
     own_rows = rows // POOL
     all_rows = n * own_rows
-    pieces = 2 + cut(block // 2, 2) + cut(block // 2, PAIRS)
+    pieces = len(pieces_of(block)[0])
     dma = pltpu.SemaphoreType.DMA
     vmem = pl.BlockSpec(memory_space=pltpu.VMEM)
     anywhere = pl.BlockSpec(memory_space=pl.ANY)
@@ -467,7 +529,7 @@
         out_specs=(vmem, vmem),
         scratch_shapes=[
             pltpu.VMEM((depth, DK), BF16),
-            pltpu.VMEM((depth, DV), BF16),
+            pltpu.VMEM((n, DV, block), BF16),
             pltpu.VMEM((depth, H * DK), BF16),
             pltpu.VMEM((depth, out_weight.shape[1]), BF16),
             pltpu.VMEM(pair_in_weight.shape, BF16),
@@ -487,12 +549,13 @@
             pltpu.VMEM((n, 16, pair_width), BF16),
             pltpu.VMEM((all_rows, pair_width), F32),
             pltpu.VMEM((own_rows * all_rows, pair_width), BF16),
+            pltpu.VMEM((2, channels), F32),
             dma((4,)),
             dma((6,)),
             dma((2, 4)),
         ]
-        + [dma((chips - 1, pieces))] * 8
-        + [dma((n - 1, 2))] * 2
+        + [dma((8, chips - 1, pieces))] * 2
+        + [dma((2 * chips - 1, 2))] * 2
         + [dma((n - 1,))] * 2,
         compiler_params=pltpu.CompilerParams(
             collective_id=0, has_side_effects=True, vmem_limit_bytes=56 * 1024 * 1024
@@ -501,12 +564,12 @@
         tower,
         dna,
         dna_weight,
-        conv_gain.reshape(1, channels),
+        conv_gain,
         depthwise_kernel,
-        attn_gain.reshape(1, channels),
+        attn_gain,
         query_weight,
         key_weight,
-        value_weight,
+        value_weight.T,
         out_weight,
         pair_in_weight,
         pair_weight,

time: 66.1 us -> 44.2 us (0.67)
  Pallas kernels: 58.2 us -> 40.7 us
  local copies, waits for them, and re-layouts: 6.93 us -> 2.62 us
    pallas_call x1, Pallas kernels: 58.2 us -> 40.7 us  [local(): pl.pallas_call(functools.partial(kernel, n), out_shape=(jax.ShapeDtypeStr...]
    reshape x2 -> x0, local copies, waits for them, and re-layouts: 2.59 us -> none  [the longest x1 1.3 us: local(): attn_gain.reshape(1, channels)]
    unnamed x5 -> x4, local copies, waits for them, and re-layouts: 4.34 us -> 2.62 us
where the time goes in v2:
time: 44.2 us; the launch traced here: 44 us
  Pallas kernels  40.7 us (92%)
  local copies, waits for them, and re-layouts  2.62 us (6%)
  between operations  0.65 us (1%)
    pallas_call x1, Pallas kernels, local(): pl.pallas_call(functools.partial(kernel, n), out_shape=(jax.ShapeDtypeStr...  40.7 us
    unnamed x4, local copies, waits for them, and re-layouts  2.62 us

profile of v2, /device:TPU:0, one launch (start us, length us, event | category | flops | bytes accessed | tf_op | source)
XLA Modules:
  0.0 44.0 jit_solution(4225353583197305804)
XLA Ops:
  0.6 40.7 %shard_map.131 = (bf16[192,1536]{1,0:T(8,128)(2,1)}, bf16[12,48,128]{2,1,0:T(8,128)(2,1)}) custom-call(bf16[192,1536]{1,0:T(8,128)(2,1)} %tower.1, s32[192,128]{1,0:T(8,128)} %dna.1, f32[4,1536]{1,0:T(4,128)} %dna_weight.1, f32[1536]{0:T(1024)} %conv_gain.1, f32[5,1536]{1,0:T(8,128)} %taps.1, f32[1536]{0:T(1024)} %attn_gain.1, bf16[384,1024]{1,0:T(8,128)(2,1)} %query_hbm.1, ...), custom_call_target="tpu_custom_call" | custom-call | tf_op jit(solution)/shard_map/pallas_call | solution.py:522
  41.4 0.0 copy-start
  41.4 2.0 %copy.16 = bf16[192,1536]{1,0:T(8,128)(2,1)} copy(bf16[192,1536]{1,0:T(8,128)(2,1)} %get-tuple-element.4) | data formatting | bytes 1179648
  43.3 0.0 copy-done
  43.3 0.7 %copy.17 = bf16[12,48,128]{2,1,0:T(8,128)(2,1)} copy(bf16[12,48,128]{2,1,0:T(8,128)(2,1)S(1)} %copy-done) | data formatting | bytes 294912
Async XLA Ops:
  41.4 2.0 %copy-start = (bf16[12,48,128]{2,1,0:T(8,128)(2,1)S(1)}, bf16[12,48,128]{2,1,0:T(8,128)(2,1)}, u32[]{:S(2)}) copy-start(bf16[12,48,128]{2,1,0:T(8,128)(2,1)} %get-tuple-element.5) | copy-start | bytes 442372
